TPU v7x, 512 devices: a whole 4x8x8 slice. The times are simulated.
512 devices in a mesh: node: 64 (over y_hi, z, core), local: 8 (over x, y_lo).
Axes of the slice: x: 4, y: 8 (y_hi: 4, y_lo: 2; y = y_hi * 2 + y_lo), z: 8, core: 2. Of those that a mesh axis runs over, the one named last changes fastest.
Arguments:
- tokens: bfloat16 [81920, 4096], P(('node', 'local')), may hold values from -24 to 24
- out_grad: bfloat16 [81920, 4096], P(('node', 'local')), may hold values from -24 to 24
- up_codes: bfloat16 [4096, 256], P('local'), may hold values from -127 to 127
- up_scales: float32 [4096, 2], P('local'), may hold values from 0.000109375 to 0.0004375
- down_codes: bfloat16 [4096, 256], P('local'), may hold values from -127 to 127
- down_scales: float32 [4096, 2], P('local'), may hold values from 0.000109375 to 0.0004375
Outputs:
- input_grad: bfloat16 [81920, 4096], P(('node', 'local'))
- grad_up: float32 [4096, 256], P(('local', 'node'))
- grad_down: float32 [4096, 256], P(('local', 'node'))
All inputs are finite; a program needn't handle non-finite values.
Results may differ from a plain program's by a relative error of at most 0.0075.
Values sent between devices are 32-bit elements; how exact they have to be, the bound alone decides.
No kernel may reach another device: no remote copies, remote signals or barrier semaphores. Data moves between devices by JAX's collectives and lax.ppermute only.
A program may use at most 128 MiB of HBM per device.

v0:
```python
import jax
import jax.numpy as jnp
from jax import lax
from jax.sharding import PartitionSpec as P

QBLOCK = 128


def side_by_side(arrays, axis, split_dim, concat_dim, along):
    widths = [a.shape[along] for a in arrays]
    both = jnp.concatenate(arrays, axis=along)
    whole = lax.all_to_all(both, axis, split_axis=split_dim, concat_axis=concat_dim, tiled=True)
    return tuple(jnp.split(whole, [sum(widths[:k]) for k in range(1, len(widths))], axis=along))


def gelu_tanh(values):
    return jax.nn.gelu(values, approximate=True)


def quantize(values):
    blocks = values.reshape(values.shape[:-1] + (values.shape[-1] // QBLOCK, QBLOCK))
    scales = 2.0 * jnp.sqrt(jnp.mean(blocks * blocks, axis=-1) + 1e-06) / 7.0
    block_codes = (
        jnp.clip(blocks / scales[..., None], -7.0, 7.0).astype(jnp.bfloat16).reshape(values.shape)
    )
    return (block_codes, scales)


def restore(block_codes, scales):
    blocks = block_codes.reshape(block_codes.shape[:-1] + (scales.shape[-1], -1))
    return (blocks * scales[..., None]).reshape(block_codes.shape)


def local(tokens, out_grad, up_codes, up_scales, down_codes, down_scales):
    gathered = (
        lax.all_gather(up_codes.astype(jnp.float32), "local", axis=0, tiled=True),
        lax.all_gather(up_scales, "local", axis=0, tiled=True),
        lax.all_gather(down_codes.astype(jnp.float32), "local", axis=0, tiled=True),
        lax.all_gather(down_scales, "local", axis=0, tiled=True),
    )
    up = restore(gathered[0], gathered[1]).astype(jnp.bfloat16)
    down = restore(gathered[2], gathered[3]).astype(jnp.bfloat16)
    preact = jnp.dot(tokens, up, preferred_element_type=jnp.float32)
    activated, slope_fn = jax.vjp(gelu_tanh, preact)
    activated = activated.astype(jnp.bfloat16)
    back_grad = jnp.dot(out_grad, down, preferred_element_type=jnp.float32)
    hidden_grad = slope_fn(back_grad)[0].astype(jnp.bfloat16)
    contract_rows = (((0,), (0,)), ((), ()))
    input_grad = lax.dot_general(
        hidden_grad, up, (((1,), (1,)), ((), ())), preferred_element_type=jnp.float32
    ).astype(jnp.bfloat16)
    first = lax.dot_general(tokens, hidden_grad, contract_rows, preferred_element_type=jnp.float32)
    second = lax.dot_general(out_grad, activated, contract_rows, preferred_element_type=jnp.float32)
    block_codes, scales = quantize(jnp.stack([first, second]))
    wide_codes = block_codes.astype(jnp.float32)
    devices_all = lax.axis_size("node") * lax.axis_size("local")
    received = (
        lax.all_to_all(wide_codes[None], "local", split_axis=2, concat_axis=0, tiled=True),
        lax.all_to_all(scales[None], "local", split_axis=2, concat_axis=0, tiled=True),
    )
    summed = jnp.sum(restore(received[0], received[1]), axis=0)
    node_codes, node_scales = quantize(summed)
    owned = side_by_side((node_codes.astype(jnp.float32)[None], node_scales[None]), "node", 2, 0, 3)
    reduced = jnp.sum(restore(owned[0], owned[1]), axis=0) / devices_all
    return (input_grad, reduced[0], reduced[1])


def solution(mesh):
    placed = (
        P(("node", "local"), None),
        P(("node", "local"), None),
        P("local", None),
        P("local", None),
        P("local", None),
        P("local", None),
    )
    return jax.shard_map(
        local,
        mesh=mesh,
        in_specs=placed,
        out_specs=(
            P(("node", "local"), None),
            P(("local", "node"), None),
            P(("local", "node"), None),
        ),
        check_vma=False,
    )
```

profile of v0, /device:TPU:1, one launch (start us, length us, event | category | flops | bytes accessed | tf_op | source)
XLA Modules:
  0.0 456.9 jit_solution(1883866873123119075)
XLA Ops:
  7.2 1.9 convert_element_type.65
  9.1 0.0 all-gather.3.cloned.1.call-start
  9.2 1.8 convert_element_type.63
  11.0 22.8 %all_gather.13 = f32[4096,2]{0,1:T(2,128)S(1)} all-gather(f32[512,2]{0,1:T(2,128)} %param.11), channel_id=1, replica_groups=mesh['node'=64,'local'=8] {'local'}, dimensions={0}, use_global_device_ids=true | all-gather | bytes 36864 | tf_op jit(solution)/shard_map/all_gather | solution.py:39
  33.8 2.0 copy.19
  35.7 23.7 %all_gather.15 = f32[4096,2]{0,1:T(2,128)S(1)} all-gather(f32[512,2]{0,1:T(2,128)S(1)} %copy-done.10), channel_id=1, replica_groups=mesh['node'=64,'local'=8] {'local'}, dimensions={0}, use_global_device_ids=true | all-gather | bytes 36864 | tf_op jit(solution)/shard_map/all_gather | solution.py:37
  59.4 0.6 copy.20
  60.1 52.7 %all-gather.5.cloned.1.call-done = f32[4096,256]{1,0:T(8,128)} async-done(((f32[512,256]{1,0:T(8,128)}), f32[4096,256]{1,0:T(8,128)}) %all-gather.5.cloned.1.call-update) | async-done | bytes 4194320 | tf_op jit(solution)/shard_map/all_gather | solution.py:36
  112.7 9.4 %mul.106 = f32[4096,2,128]{2,1,0:T(2,128)S(1)} broadcast(f32[4096,2]{1,0:T(8,128)S(1)} %copy.20), dimensions={0,1} | broadcast | bytes 4227072 | tf_op jit(solution)/shard_map/mul | solution.py:31
  122.2 0.8 fusion.5
  123.0 0.5 copy-done.4
  123.5 0.6 convolution_bitcast_fusion
  124.1 0.7 copy-done.8
  124.7 2.7 fusion.25
  127.5 83.5 %all-gather.3.cloned.1.call-done = f32[4096,256]{1,0:T(8,128)} async-done(((f32[512,256]{1,0:T(8,128)}), f32[4096,256]{1,0:T(8,128)}) %all-gather.3.cloned.1.call-update) | async-done | bytes 4194320 | tf_op jit(solution)/shard_map/all_gather | solution.py:38
  211.0 8.7 %mul.103 = f32[4096,2,128]{2,1,0:T(2,128)S(1)} broadcast(f32[4096,2]{1,0:T(8,128)} %copy.19), dimensions={0,1} | broadcast | bytes 4227072 | tf_op jit(solution)/shard_map/mul | solution.py:31
  219.7 0.8 fusion.22
  220.5 0.5 copy-done.5
  221.0 0.7 fusion.37
  221.7 2.7 copy-done.2
  224.4 0.8 fusion.2
  225.2 0.1 sqrt_multiply_fusion
  225.4 4.3 copy.23
  229.7 8.1 %reshape.171 = f32[8,1,2048]{2,1,0:T(1,128)} reshape(f32[4096,1,2,2]{3,2,1,0:T(2,128)} %bitcast.94) | data formatting | bytes 131072
  237.8 3.8 all-to-all-start.1
  241.6 6.3 %fusion.4 = f32[1,2,4096,256]{2,3,1,0:T(8,128)} fusion(f32[1,1,4096,256]{2,3,1,0:T(8,128)} %bitcast.87, f32[1,1,4096,256]{2,3,1,0:T(8,128)} %bitcast.90, f32[2,4096,2]{1,2,0:T(2,128)S(1)} %get-tuple-element.3), kind=kLoop, calls=%fused_computation.8 | loop fusion | flops 10485760 | bytes 16842752 | tf_op jit(solution)/shard_map/convert_element_type | solution.py:55
  247.9 13.2 %copy.21 = f32[1,2,4096,256]{3,1,0,2:T(2,128)} copy(f32[1,2,4096,256]{2,3,1,0:T(8,128)} %fusion.4) | data formatting | bytes 16777216 | tf_op jit(solution)/shard_map/convert_element_type | solution.py:55
  261.1 5.1 %all-to-all-start = ((f32[1,2,4096,256]{3,1,0,2:T(2,128)}), f32[1,2,4096,256]{3,1,0,2:T(2,128)}, u32[]{:S(2)}, u32[]{:S(2)}) async-start(f32[1,2,4096,256]{3,1,0,2:T(2,128)} %copy.21), calls=%async_computation | async-start | bytes 16777216 | tf_op jit(solution)/shard_map/all_to_all | solution.py:58
  266.2 0.5 broadcast.163
  266.8 0.8 reduce
  267.6 8.4 %reshape.172 = f32[4096,1,2,2]{3,2,1,0:T(2,128)} reshape(f32[8,2048]{1,0:T(8,128)S(1)} %reduce) | data formatting | bytes 131072
  275.9 3.5 copy.24
  279.5 79.8 %all-to-all-done = f32[1,2,4096,256]{3,1,0,2:T(2,128)} async-done(((f32[1,2,4096,256]{3,1,0,2:T(2,128)}), f32[1,2,4096,256]{3,1,0,2:T(2,128)}, u32[]{:S(2)}, u32[]{:S(2)}) %all-to-all-start) | async-done | bytes 8388640 | tf_op jit(solution)/shard_map/all_to_all | solution.py:58
  359.3 10.0 %copy.22 = f32[1,2,8,512,256]{3,2,4,1,0:T(8,128)} copy(f32[1,2,8,512,256]{4,1,3,2,0:T(2,128)} %bitcast.9) | data formatting | bytes 16777216 | tf_op jit(solution)/shard_map/all_to_all | solution.py:58
  369.2 4.3 mul.126
  373.5 9.9 %fusion.3 = f32[2,512,256]{1,2,0:T(8,128)S(1)} fusion(f32[8,2,512,256]{2,0,3,1:T(8,128)} %bitcast.91, f32[1,2,8,512,256]{3,2,4,1,0:T(8,128)} %copy.22), kind=kLoop, calls=%fused_computation.6 | loop fusion | flops 3932160 | bytes 17825792 | tf_op jit(solution)/shard_map/reduce_sum | solution.py:61
  383.4 0.1 bitcast_reduce_fusion
  383.5 0.1 fusion.15
  383.7 0.1 pad_maximum_fusion
  383.8 2.2 copy.25
  386.0 15.4 %all-to-all-start.2 = ((f32[1,2,512,258]{3,1,0,2:T(2,128)}), f32[1,2,512,258]{3,1,0,2:T(2,128)}, u32[]{:S(2)}, u32[]{:S(2)}) async-start(f32[1,2,512,258]{3,1,0,2:T(2,128)} %copy.25), calls=%async_computation.2 | async-start | bytes 3145728 | tf_op jit(solution)/shard_map/all_to_all | solution.py:12
  401.5 1.9 convolution_convert_fusion
  403.4 40.5 %all-to-all-done.2 = f32[1,2,512,258]{3,1,0,2:T(2,128)} async-done(((f32[1,2,512,258]{3,1,0,2:T(2,128)}), f32[1,2,512,258]{3,1,0,2:T(2,128)}, u32[]{:S(2)}, u32[]{:S(2)}) %all-to-all-start.2) | async-done | bytes 1056800 | tf_op jit(solution)/shard_map/all_to_all | solution.py:12
  443.9 1.1 split.9
  444.9 1.2 mul.131
  446.2 1.2 mul.132
  447.4 2.0 fusion.12
  449.5 0.6 copy_bitcast_fusion
  (25 shorter events, 0.2 us)
Async XLA Ops:
  7.2 117.6 %copy-start = (bf16[160,4096]{1,0:T(8,128)(2,1)S(1)}, bf16[160,4096]{1,0:T(8,128)(2,1)}, u32[]{:S(2)}) copy-start(bf16[160,4096]{1,0:T(8,128)(2,1)} %param.7) | copy-start | bytes 3932164
  7.2 28.6 %copy-start.10 = (f32[512,2]{0,1:T(2,128)S(1)}, f32[512,2]{0,1:T(2,128)}, u32[]{:S(2)}) copy-start(f32[512,2]{0,1:T(2,128)} %param.9) | copy-start | bytes 12292
  7.2 105.5 %all-gather.5.cloned.1.call-start = ((), (), s32[]{:S(2)}) async-start(), calls=%async_computation.4 | async-start | bytes 4718592 | tf_op jit(solution)/shard_map/all_gather | solution.py:36
  9.1 201.8 %all-gather.3.cloned.1.call-start = ((), (), s32[]{:S(2)}) async-start(), calls=%async_computation.3 | async-start | bytes 4718592 | tf_op jit(solution)/shard_map/all_gather | solution.py:38
  112.7 9.4 %copy-start.7 = (f32[4096,256]{1,0:T(8,128)S(1)}, f32[4096,256]{1,0:T(8,128)}, u32[]{:S(2)}) copy-start(f32[4096,256]{1,0:T(8,128)} %all-gather.5.cloned.1.call-done) | copy-start | bytes 12582916
  122.2 1.3 copy-start.4
  124.1 0.7 copy-start.8
  211.0 8.7 %copy-start.6 = (f32[4096,256]{1,0:T(8,128)S(1)}, f32[4096,256]{1,0:T(8,128)}, u32[]{:S(2)}) copy-start(f32[4096,256]{1,0:T(8,128)} %all-gather.3.cloned.1.call-done) | copy-start | bytes 12582916
  211.0 8.7 %copy-start.9 = (f32[160,256]{1,0:T(8,128)S(1)}, f32[160,256]{1,0:T(8,128)}, u32[]{:S(2)}) copy-start(f32[160,256]{1,0:T(8,128)} %copy-done.8) | copy-start | bytes 491524
  219.7 1.3 copy-start.5
  221.0 3.5 copy-start.2
  221.7 3.5 copy-start.3
  237.8 23.3 %all-to-all-start.1 = ((f32[8,1,2048]{2,1,0:T(1,128)}), f32[8,1,2048]{2,1,0:T(1,128)S(1)}, u32[]{:S(2)}, u32[]{:S(2)}) async-start(f32[8,1,2048]{2,1,0:T(1,128)} %reshape.171), calls=%async_computation.1 | async-start | bytes 131072 | tf_op jit(solution)/shard_map/all_to_all | solution.py:59
  261.1 98.2 %all-to-all-start = ((f32[1,2,4096,256]{3,1,0,2:T(2,128)}), f32[1,2,4096,256]{3,1,0,2:T(2,128)}, u32[]{:S(2)}, u32[]{:S(2)}) async-start(f32[1,2,4096,256]{3,1,0,2:T(2,128)} %copy.21), calls=%async_computation | async-start | bytes 16777216 | tf_op jit(solution)/shard_map/all_to_all | solution.py:58
  386.0 57.9 %all-to-all-start.2 = ((f32[1,2,512,258]{3,1,0,2:T(2,128)}), f32[1,2,512,258]{3,1,0,2:T(2,128)}, u32[]{:S(2)}, u32[]{:S(2)}) async-start(f32[1,2,512,258]{3,1,0,2:T(2,128)} %copy.25), calls=%async_computation.2 | async-start | bytes 3145728 | tf_op jit(solution)/shard_map/all_to_all | solution.py:12
  401.5 48.6 %copy-start.1 = (bf16[160,4096]{1,0:T(8,128)(2,1)S(1)}, bf16[160,4096]{1,0:T(8,128)(2,1)}, u32[]{:S(2)}) copy-start(bf16[160,4096]{1,0:T(8,128)(2,1)} %param.7) | copy-start | bytes 3932164
Sparse Core Ops, SparseCore 0:
  10.7 102.0 all-gather.4
  114.8 96.1 all-gather.2
where the time goes:
time: 458 us; the launch traced here: 457 us
  waiting for transfers between devices  256 us (56%)
  local copies, waits for them, and re-layouts  83.8 us (18%)
  blocking collectives  46.5 us (10%)
  other arithmetic  24.7 us (5%)
  starting transfers between devices  24.5 us (5%)
  between operations  14.3 us (3%)
  matrix products  6.67 us (1%)
    all_gather x1, waiting for transfers between devices, local(): lax.all_gather(down_codes.astype(jnp.float32), 'local', axis=0, tiled=True)  83.5 us
    all_to_all x1, waiting for transfers between devices, local(): lax.all_to_all(wide_codes[None], 'local', split_axis=2, concat_axis=0, ti...  79.8 us
    all_gather x1, waiting for transfers between devices, local(): lax.all_gather(up_codes.astype(jnp.float32), 'local', axis=0, tiled=True)  52.7 us
    all_to_all x1, waiting for transfers between devices, side_by_side(): lax.all_to_all(both, axis, split_axis=split_dim, concat_axis=concat_dim,...  40.5 us
    mul x6, local copies, waits for them, and re-layouts, restore(): return (blocks * scales[..., None]).reshape(block_codes.shape)  28.4 us
    all_gather x1, blocking collectives, local(): lax.all_gather(up_scales, 'local', axis=0, tiled=True)  23.7 us
    all_gather x1, blocking collectives, local(): lax.all_gather(down_scales, 'local', axis=0, tiled=True)  22.8 us
    unnamed x25, local copies, waits for them, and re-layouts  21.5 us
  transfers between devices with their start and end apart: 5, of which 4 were waited for; matrix products, arithmetic and copies ran while one was open for 11% of the time, Pallas kernels for 0%

commit v1 on v0

--- a/solution.py
+++ b/solution.py
@@ -55,7 +55,15 @@
     wide_codes = block_codes.astype(jnp.float32)
     devices_all = lax.axis_size("node") * lax.axis_size("local")
     received = (
-        lax.all_to_all(wide_codes[None], "local", split_axis=2, concat_axis=0, tiled=True),
+        jnp.concatenate(
+            lax.all_to_all(
+                jnp.stack(jnp.split(wide_codes[None], lax.axis_size("local"), axis=2)),
+                "local",
+                0,
+                0,
+            ),
+            axis=0,
+        ),
         lax.all_to_all(scales[None], "local", split_axis=2, concat_axis=0, tiled=True),
     )
     summed = jnp.sum(restore(received[0], received[1]), axis=0)

time: 458 us -> 431 us (0.941)
  local copies, waits for them, and re-layouts: 83.8 us -> 65.3 us
  other arithmetic: 24.7 us -> 17.2 us
    convert_element_type x1 -> x0, local copies, waits for them, and re-layouts: 13.2 us -> none  [local(): wide_codes = block_codes.astype(jnp.float32)]
    all_to_all x1 -> x0, local copies, waits for them, and re-layouts: 9.95 us -> none  [local(): lax.all_to_all(wide_codes[None], 'local', split_axis=2, concat_axis=0, ti...]
    mul x6 -> x5, local copies, waits for them, and re-layouts: 28.4 us -> 20.6 us  [restore(): return (blocks * scales[..., None]).reshape(block_codes.shape)]
    unnamed x25 -> x32, local copies, waits for them, and re-layouts: 21.5 us -> 29.2 us
    reduce_sum x1, other arithmetic: 9.89 us -> 4.62 us  [local(): summed = jnp.sum(restore(received[0], received[1]), axis=0)]
where the time goes in v1:
time: 431 us
  waiting for transfers between devices  256 us (59%)
  local copies, waits for them, and re-layouts  65.3 us (15%)
  blocking collectives  46.4 us (11%)
  starting transfers between devices  24.5 us (6%)
  other arithmetic  17.2 us (4%)
  between operations  14.3 us (3%)
  matrix products  6.67 us (2%)
    all_gather x1, waiting for transfers between devices, local(): lax.all_gather(down_codes.astype(jnp.float32), 'local', axis=0, tiled=True)  83.5 us
    all_to_all x1, waiting for transfers between devices, local(): lax.all_to_all(jnp.stack(jnp.split(wide_codes[None], lax.axis_size('local...  79.7 us
    all_gather x1, waiting for transfers between devices, local(): lax.all_gather(up_codes.astype(jnp.float32), 'local', axis=0, tiled=True)  52.7 us
    all_to_all x1, waiting for transfers between devices, side_by_side(): lax.all_to_all(both, axis, split_axis=split_dim, concat_axis=concat_dim,...  40.4 us
    unnamed x32, local copies, waits for them, and re-layouts  29.2 us
    all_gather x1, blocking collectives, local(): lax.all_gather(up_scales, 'local', axis=0, tiled=True)  23.6 us
    all_gather x1, blocking collectives, local(): lax.all_gather(down_scales, 'local', axis=0, tiled=True)  22.8 us
    mul x5, local copies, waits for them, and re-layouts, restore(): return (blocks * scales[..., None]).reshape(block_codes.shape)  20.6 us
  transfers between devices with their start and end apart: 5, of which 4 were waited for; matrix products, arithmetic and copies ran while one was open for 11% of the time, Pallas kernels for 0%

profile of v1, /device:TPU:1, one launch (start us, length us, event | category | flops | bytes accessed | tf_op | source)
XLA Modules:
  0.0 430.6 jit_solution(9437788747166800616)
XLA Ops:
  7.2 1.9 convert_element_type.65
  9.2 1.8 convert_element_type.63
  11.0 22.8 %all_gather.13 = f32[4096,2]{0,1:T(2,128)S(1)} all-gather(f32[512,2]{0,1:T(2,128)} %param.11), channel_id=1, replica_groups=mesh['node'=64,'local'=8] {'local'}, dimensions={0}, use_global_device_ids=true | all-gather | bytes 36864 | tf_op jit(solution)/shard_map/all_gather | solution.py:39
  33.8 2.0 copy.22
  35.8 23.6 %all_gather.15 = f32[4096,2]{0,1:T(2,128)S(1)} all-gather(f32[512,2]{0,1:T(2,128)S(1)} %copy-done.10), channel_id=1, replica_groups=mesh['node'=64,'local'=8] {'local'}, dimensions={0}, use_global_device_ids=true | all-gather | bytes 36864 | tf_op jit(solution)/shard_map/all_gather | solution.py:37
  59.4 0.6 copy.23
  60.1 52.7 %all-gather.5.cloned.1.call-done = f32[4096,256]{1,0:T(8,128)} async-done(((f32[512,256]{1,0:T(8,128)}), f32[4096,256]{1,0:T(8,128)}) %all-gather.5.cloned.1.call-update) | async-done | bytes 4194320 | tf_op jit(solution)/shard_map/all_gather | solution.py:36
  112.7 9.4 %mul.106 = f32[4096,2,128]{2,1,0:T(2,128)S(1)} broadcast(f32[4096,2]{1,0:T(8,128)S(1)} %copy.23), dimensions={0,1} | broadcast | bytes 4227072 | tf_op jit(solution)/shard_map/mul | solution.py:31
  122.2 0.8 fusion.5
  123.0 0.5 copy-done.4
  123.5 0.6 convolution_bitcast_fusion
  124.1 0.7 copy-done.8
  124.7 2.7 fusion.33
  127.4 83.5 %all-gather.3.cloned.1.call-done = f32[4096,256]{1,0:T(8,128)} async-done(((f32[512,256]{1,0:T(8,128)}), f32[4096,256]{1,0:T(8,128)}) %all-gather.3.cloned.1.call-update) | async-done | bytes 4194320 | tf_op jit(solution)/shard_map/all_gather | solution.py:38
  211.0 8.7 %mul.103 = f32[4096,2,128]{2,1,0:T(2,128)S(1)} broadcast(f32[4096,2]{1,0:T(8,128)} %copy.22), dimensions={0,1} | broadcast | bytes 4227072 | tf_op jit(solution)/shard_map/mul | solution.py:31
  219.7 0.8 fusion.30
  220.5 0.5 copy-done.5
  221.0 0.7 fusion.45
  221.7 2.7 copy-done.2
  224.4 0.8 fusion.2
  225.4 4.4 %copy.24 = f32[1,2,4096,2]{3,1,0,2:T(2,128)} copy(f32[1,2,4096,2]{2,3,1,0:T(2,128)S(1)} %get-tuple-element.3) | data formatting | bytes 131072 | tf_op jit(solution)/shard_map/div | solution.py:22
  229.7 8.1 %reshape.166 = f32[8,1,2048]{2,1,0:T(1,128)} reshape(f32[4096,1,2,2]{3,2,1,0:T(2,128)} %bitcast.122) | data formatting | bytes 131072
  237.9 3.8 all-to-all-start.1
  241.7 4.0 fusion.4
  245.7 1.2 fusion.20
  246.8 1.1 fusion.19
  247.9 1.1 fusion.18
  249.0 1.1 fusion.17
  250.1 1.2 fusion.16
  251.2 1.1 fusion.15
  252.3 1.1 fusion.14
  253.4 1.1 fusion.13
  254.4 5.1 %all-to-all-start = ((f32[8,1,2,512,256]{3,4,2,1,0:T(8,128)}), f32[8,1,2,512,256]{3,4,2,1,0:T(8,128)}, u32[]{:S(2)}, u32[]{:S(2)}) async-start(f32[8,1,2,512,256]{3,4,2,1,0:T(8,128)} %fusion.13), calls=%async_computation | async-start | bytes 16777216 | tf_op jit(solution)/shard_map/all_to_all | solution.py:59
  259.6 0.5 broadcast.163
  260.1 0.8 reduce
  260.9 8.4 %reshape.167 = f32[4096,1,2,2]{3,2,1,0:T(2,128)} reshape(f32[8,2048]{1,0:T(8,128)S(1)} %reduce) | data formatting | bytes 131072
  269.3 3.5 copy.28
  272.9 79.7 %all-to-all-done = f32[8,1,2,512,256]{3,4,2,1,0:T(8,128)} async-done(((f32[8,1,2,512,256]{3,4,2,1,0:T(8,128)}), f32[8,1,2,512,256]{3,4,2,1,0:T(8,128)}, u32[]{:S(2)}, u32[]{:S(2)}) %all-to-all-start) | async-done | bytes 8388640 | tf_op jit(solution)/shard_map/all_to_all | solution.py:59
  352.6 4.6 %fusion.3 = f32[2,512,256]{1,2,0:T(8,128)S(1)} fusion(f32[8,1,2,512,256]{3,4,2,1,0:T(8,128)} %all-to-all-done, f32[8,2,512,2]{2,3,1,0:T(2,128)S(1)} %copy.26), kind=kLoop, calls=%fused_computation.6 | loop fusion | flops 3932160 | bytes 9502720 | tf_op jit(solution)/shard_map/reduce_sum | solution.py:69
  357.6 2.2 copy.27
  359.8 15.4 %all-to-all-start.2 = ((f32[1,2,512,258]{3,1,0,2:T(2,128)}), f32[1,2,512,258]{3,1,0,2:T(2,128)}, u32[]{:S(2)}, u32[]{:S(2)}) async-start(f32[1,2,512,258]{3,1,0,2:T(2,128)} %copy.27), calls=%async_computation.2 | async-start | bytes 3145728 | tf_op jit(solution)/shard_map/all_to_all | solution.py:12
  375.3 1.9 convolution_convert_fusion
  377.2 40.4 %all-to-all-done.2 = f32[1,2,512,258]{3,1,0,2:T(2,128)} async-done(((f32[1,2,512,258]{3,1,0,2:T(2,128)}), f32[1,2,512,258]{3,1,0,2:T(2,128)}, u32[]{:S(2)}, u32[]{:S(2)}) %all-to-all-start.2) | async-done | bytes 1056800 | tf_op jit(solution)/shard_map/all_to_all | solution.py:12
  417.6 1.1 split.49
  418.7 1.2 mul.131
  419.9 1.2 mul.132
  421.1 2.0 fusion.12
  423.2 0.6 copy_bitcast_fusion
  (31 shorter events, 0.7 us)
Async XLA Ops:
  7.2 117.6 %copy-start = (bf16[160,4096]{1,0:T(8,128)(2,1)S(1)}, bf16[160,4096]{1,0:T(8,128)(2,1)}, u32[]{:S(2)}) copy-start(bf16[160,4096]{1,0:T(8,128)(2,1)} %param.7) | copy-start | bytes 3932164
  7.2 28.6 %copy-start.10 = (f32[512,2]{0,1:T(2,128)S(1)}, f32[512,2]{0,1:T(2,128)}, u32[]{:S(2)}) copy-start(f32[512,2]{0,1:T(2,128)} %param.9) | copy-start | bytes 12292
  7.2 105.5 %all-gather.5.cloned.1.call-start = ((), (), s32[]{:S(2)}) async-start(), calls=%async_computation.4 | async-start | bytes 4718592 | tf_op jit(solution)/shard_map/all_gather | solution.py:36
  9.1 201.8 %all-gather.3.cloned.1.call-start = ((), (), s32[]{:S(2)}) async-start(), calls=%async_computation.3 | async-start | bytes 4718592 | tf_op jit(solution)/shard_map/all_gather | solution.py:38
  112.7 9.4 %copy-start.7 = (f32[4096,256]{1,0:T(8,128)S(1)}, f32[4096,256]{1,0:T(8,128)}, u32[]{:S(2)}) copy-start(f32[4096,256]{1,0:T(8,128)} %all-gather.5.cloned.1.call-done) | copy-start | bytes 12582916
  122.2 1.3 copy-start.4
  124.1 0.7 copy-start.8
  211.0 8.7 %copy-start.6 = (f32[4096,256]{1,0:T(8,128)S(1)}, f32[4096,256]{1,0:T(8,128)}, u32[]{:S(2)}) copy-start(f32[4096,256]{1,0:T(8,128)} %all-gather.3.cloned.1.call-done) | copy-start | bytes 12582916
  211.0 8.7 %copy-start.9 = (f32[160,256]{1,0:T(8,128)S(1)}, f32[160,256]{1,0:T(8,128)}, u32[]{:S(2)}) copy-start(f32[160,256]{1,0:T(8,128)} %copy-done.8) | copy-start | bytes 491524
  219.7 1.3 copy-start.5
  221.0 3.5 copy-start.2
  221.7 3.5 copy-start.3
  237.9 16.6 %all-to-all-start.1 = ((f32[8,1,2048]{2,1,0:T(1,128)}), f32[8,1,2048]{2,1,0:T(1,128)S(1)}, u32[]{:S(2)}, u32[]{:S(2)}) async-start(f32[8,1,2048]{2,1,0:T(1,128)} %reshape.166), calls=%async_computation.1 | async-start | bytes 131072 | tf_op jit(solution)/shard_map/all_to_all | solution.py:67
  254.4 98.2 %all-to-all-start = ((f32[8,1,2,512,256]{3,4,2,1,0:T(8,128)}), f32[8,1,2,512,256]{3,4,2,1,0:T(8,128)}, u32[]{:S(2)}, u32[]{:S(2)}) async-start(f32[8,1,2,512,256]{3,4,2,1,0:T(8,128)} %fusion.13), calls=%async_computation | async-start | bytes 16777216 | tf_op jit(solution)/shard_map/all_to_all | solution.py:59
  359.8 57.7 %all-to-all-start.2 = ((f32[1,2,512,258]{3,1,0,2:T(2,128)}), f32[1,2,512,258]{3,1,0,2:T(2,128)}, u32[]{:S(2)}, u32[]{:S(2)}) async-start(f32[1,2,512,258]{3,1,0,2:T(2,128)} %copy.27), calls=%async_computation.2 | async-start | bytes 3145728 | tf_op jit(solution)/shard_map/all_to_all | solution.py:12
  375.3 48.5 %copy-start.1 = (bf16[160,4096]{1,0:T(8,128)(2,1)S(1)}, bf16[160,4096]{1,0:T(8,128)(2,1)}, u32[]{:S(2)}) copy-start(bf16[160,4096]{1,0:T(8,128)(2,1)} %param.7) | copy-start | bytes 3932164
Sparse Core Ops, SparseCore 0:
  10.7 102.0 all-gather.4
  114.8 96.1 all-gather.2
